TPU v7x, 32 devices: a whole 2x2x4 slice. The times are simulated.
32 devices in a mesh: grp: 2 (over y), reg: 4 (over x, core), dev: 4 (over z).
Axes of the slice: x: 2, y: 2, z: 4, core: 2. Of those that a mesh axis runs over, the one named last changes fastest.
Arguments:
- footprints: bfloat16 [4096, 128, 128], P(('grp', 'reg', 'dev')), parts along dimension 0, may hold values from 0.0009994507 to 0.029907227
- block_coords: int32 [4096, 2], P(('grp', 'reg', 'dev')), parts along dimension 0, may hold values from 0 to 127, as said below
- receptor_place: int32 [256], P('grp'), parts along dimension 0, may hold values from 0 to 127, as said below
- source_place: int32 [128], P('grp'), parts along dimension 0, may hold values from 0 to 63, as said below
- probe_matrix: bfloat16 [16384, 256], P(('grp', 'reg', 'dev')), parts along dimension 0, may hold values from -6 to 6
Outputs:
- receptor_image: bfloat16 [32768, 256], P(('grp', 'dev')), parts along dimension 0
- source_image: float32 [16384, 256], P(('grp', 'reg', 'dev')), parts along dimension 0
There are 2 independent parts, one for each index of `grp`. A program takes and returns all parts, laid end to end along the dimension named above; each array names one. Nothing has to cross between parts.
Inputs may be any that keep to these rules, and one draw needn't show every extreme that they name: `block_coords`: the destination of a block is the device whose reg index is pos_src // 16 and whose dev index is pos_rec // 32. The 128 blocks of one device send at most 16 blocks to any one destination, and one particular destination receives exactly 16 from every device (the others may receive fewer). Column 0 is below 128, column 1 below 64. `receptor_place`: A permutation of the receptor blocks. `source_place`: A permutation of the source blocks.
All inputs are finite; a program needn't handle non-finite values.
Results may differ from a plain program's by a relative error of at most 0.0085.
Values may be sent and summed in bfloat16 or wider, within the bound.
A program may use at most 128 MiB of HBM per device.

v0:
```python
import math

import jax
import jax.numpy as jnp
from jax import lax
from jax.sharding import PartitionSpec as P


def local(footprints, block_coords, receptor_place, source_place, probe_matrix):
    cells = footprints.shape[1]
    block_count = footprints.shape[0]
    columns = probe_matrix.shape[1]
    dev_count = lax.axis_size("dev")
    reg_count = lax.axis_size("reg")
    owners = reg_count * dev_count
    capacity = 2 * block_count // owners
    per_device = probe_matrix.shape[0] // cells
    region = per_device * dev_count
    receptor_tile = receptor_place.shape[0] // dev_count
    pos_rec = receptor_place[block_coords[:, 0]]
    pos_src = source_place[block_coords[:, 1]]
    target = pos_src // region * dev_count + pos_rec // receptor_tile
    same_target = target[:, None] == target[None, :]
    earlier = lax.broadcasted_iota(jnp.int32, (block_count, block_count), 1) < lax.broadcasted_iota(
        jnp.int32, (block_count, block_count), 0
    )
    rank_slot = jnp.sum((same_target & earlier).astype(jnp.int32), axis=1)
    local_index = jnp.stack([pos_rec % receptor_tile, pos_src % region], axis=1).astype(
        jnp.bfloat16
    )
    send_blocks = (
        jnp.zeros((owners, capacity, cells, cells), jnp.bfloat16)
        .at[target, rank_slot]
        .set(footprints)
    )
    send_index = (
        jnp.zeros((owners, capacity, 2), jnp.bfloat16).at[target, rank_slot].set(local_index)
    )
    got_blocks, got_index = (
        lax.all_to_all(send_blocks, ("reg", "dev"), split_axis=0, concat_axis=0, tiled=True),
        lax.all_to_all(send_index, ("reg", "dev"), split_axis=0, concat_axis=0, tiled=True),
    )
    slot_count = owners * capacity
    group_size = math.gcd(slot_count, 32)
    groups = slot_count // group_size
    grouped_blocks = got_blocks.reshape(groups, group_size, cells, cells)
    index_int = got_index.reshape(slot_count, 2).astype(jnp.int32)
    grouped_rec = index_int[:, 0].reshape(groups, group_size)
    grouped_src = index_int[:, 1].reshape(groups, group_size)
    region_probe = lax.all_gather(probe_matrix, "dev", axis=0, tiled=True).reshape(
        region, cells, columns
    )

    def forward_step(running, items):
        pieces, rec_slot, src_slot = items
        taken = region_probe[src_slot]
        terms = jnp.einsum("gij,gjk->gik", pieces, taken, preferred_element_type=jnp.float32)
        return (running.at[rec_slot].add(terms), None)

    start_rec = jnp.zeros((receptor_tile, cells, columns), jnp.float32)
    receptor_part, unused = lax.scan(
        forward_step, start_rec, (grouped_blocks, grouped_rec, grouped_src)
    )
    receptor_image = lax.psum(receptor_part, "reg").astype(jnp.bfloat16)

    def backward_step(running, items):
        pieces, rec_slot, src_slot = items
        taken = receptor_image[rec_slot]
        terms = jnp.einsum("gji,gjk->gik", pieces, taken, preferred_element_type=jnp.float32)
        return (running.at[src_slot].add(terms), None)

    start_src = jnp.zeros((region, cells, columns), jnp.float32)
    source_part, unused_two = lax.scan(
        backward_step, start_src, (grouped_blocks, grouped_rec, grouped_src)
    )
    source_image = (
        lax.psum_scatter(source_part.astype(jnp.bfloat16), "dev", scatter_dimension=0, tiled=True)
        .astype(jnp.float32)
        .reshape(per_device * cells, columns)
    )
    return (receptor_image.reshape(receptor_tile * cells, columns), source_image)


def solution(mesh):
    return jax.shard_map(
        local,
        mesh=mesh,
        in_specs=(
            P(("grp", "reg", "dev"), None, None),
            P(("grp", "reg", "dev"), None),
            P("grp"),
            P("grp"),
            P(("grp", "reg", "dev"), None),
        ),
        out_specs=(P(("grp", "dev"), None), P(("grp", "reg", "dev"), None)),
        check_vma=False,
    )
```

profile of v0, /device:TPU:0, one launch (start us, length us, event | category | flops | bytes accessed | tf_op | source)
XLA Modules:
  0.0 607.9 jit_solution(12205478321320632641)
XLA Ops:
  7.2 0.8 fusion.20
  8.0 1.2 gather_fusion.2
  9.2 1.6 gather_fusion.3
  11.2 6.9 %scatter_fusion.2 = bf16[16,16,2]{2,1,0:T(8,128)(2,1)S(1)} fusion(bf16[16,16,2]{2,1,0:T(8,128)(2,1)S(1)} %broadcast_in_dim.9, s32[128]{0:T(128)S(1)} %get-tuple-element.143, bf16[128,2]{1,0:T(8,128)(2,1)S(1)} %copy.25), kind=kCustom, calls=%fused_computation.6 | custom fusion | bytes 2560 | tf_op jit(solution)/shard_map/scatter | solution.py:37
  18.1 0.8 copy.26
  18.9 7.4 %all-to-all-start = ((bf16[16,16,2]{1,2,0:T(2,128)(2,1)}), bf16[16,16,2]{1,2,0:T(2,128)(2,1)S(1)}, u32[]{:S(2)}, u32[]{:S(2)}) async-start(bf16[16,16,2]{1,2,0:T(2,128)(2,1)} %copy.26), calls=%async_computation | async-start | bytes 16384 | tf_op jit(solution)/shard_map/all_to_all | solution.py:41
  26.3 5.3 broadcast_in_dim.10
  31.6 20.7 %scatter_fusion.3 = bf16[16,16,128,128]{3,2,1,0:T(8,128)(2,1)} fusion(bf16[16,16,128,128]{3,2,1,0:T(8,128)(2,1)} %broadcast_in_dim.10, s32[128]{0:T(128)S(1)} %get-tuple-element.143, bf16[128,128,128]{2,1,0:T(8,128)(2,1)} %param.9), kind=kCustom, calls=%fused_computation.7 | custom fusion | bytes 12583936 | tf_op jit(solution)/shard_map/scatter | solution.py:34
  52.3 6.1 all-to-all-start.1
  58.5 0.7 all-gather.2.cloned.1.call-update
  59.5 74.6 %all-gather.2.cloned.1.call-done = bf16[2048,256]{1,0:T(8,128)(2,1)} async-done(((bf16[512,256]{1,0:T(8,128)(2,1)}), bf16[2048,256]{1,0:T(8,128)(2,1)}) %all-gather.2.cloned.1.call-update) | async-done | bytes 1048592 | tf_op jit(solution)/shard_map/all_gather | solution.py:50
  134.1 125.5 %all-to-all-done.1 = bf16[16,16,128,128]{3,2,1,0:T(8,128)(2,1)} async-done(((bf16[16,16,128,128]{3,2,1,0:T(8,128)(2,1)}), bf16[16,16,128,128]{3,2,1,0:T(8,128)(2,1)}, u32[]{:S(2)}, u32[]{:S(2)}) %all-to-all-start.1) | async-done | bytes 8388640 | tf_op jit(solution)/shard_map/all_to_all | solution.py:40
  259.6 2.4 broadcast_in_dim.8
  262.0 113.7 %while.20 = (s32[]{:T(128)}, f32[32,128,256]{2,1,0:T(8,128)}, s32[8,32]{1,0:T(8,128)S(1)}, bf16[8,32,128,128]{3,2,1,0:T(8,128)(2,1)}, s32[8,32]{1,0:T(8,128)S(1)}, /*index=5*/bf16[16,128,256]{2,1,0:T(8,128)(2,1)S(1)}, s32[]{:T(128)}) while((s32[]{:T(128)}, f32[32,128,256]{2,1,0:T(8,128)}, s32[8,32]{1,0:T(8,128)S(1)}, ...), condition=%wide.region_5.6_spmd, body=%wide.region_3.5_spmd.sunk | while | flops 269485248 | bytes 24122832 | solution.py:61
  262.1 0.7 gather_fusion
  262.7 3.9 fusion.37
  266.7 9.5 %scatter_fusion = f32[32,128,256]{2,1,0:T(8,128)} fusion(f32[32,128,256]{2,1,0:T(8,128)} %get-tuple-element.237, s32[32]{0:T(128)S(1)} %get-tuple-element.219, f32[32,128,256]{2,1,0:T(8,128)} %fusion.37), kind=kCustom, calls=%fused_computation.4.clone.1 | custom fusion | flops 1048576 | bytes 12583040 | tf_op jit(solution)/shard_map/while/body/eval_jaxpr/scatter-add | solution.py:58
  276.2 0.7 gather_fusion
  276.9 3.9 fusion.37
  280.8 9.5 %scatter_fusion = f32[32,128,256]{2,1,0:T(8,128)} fusion(f32[32,128,256]{2,1,0:T(8,128)} %get-tuple-element.237, s32[32]{0:T(128)S(1)} %get-tuple-element.219, f32[32,128,256]{2,1,0:T(8,128)} %fusion.37), kind=kCustom, calls=%fused_computation.4.clone.1 | custom fusion | flops 1048576 | bytes 12583040 | tf_op jit(solution)/shard_map/while/body/eval_jaxpr/scatter-add | solution.py:58
  290.4 0.7 gather_fusion
  291.0 3.9 fusion.37
  295.0 9.5 %scatter_fusion = f32[32,128,256]{2,1,0:T(8,128)} fusion(f32[32,128,256]{2,1,0:T(8,128)} %get-tuple-element.237, s32[32]{0:T(128)S(1)} %get-tuple-element.219, f32[32,128,256]{2,1,0:T(8,128)} %fusion.37), kind=kCustom, calls=%fused_computation.4.clone.1 | custom fusion | flops 1048576 | bytes 12583040 | tf_op jit(solution)/shard_map/while/body/eval_jaxpr/scatter-add | solution.py:58
  304.5 0.7 gather_fusion
  305.1 3.9 fusion.37
  309.1 9.5 %scatter_fusion = f32[32,128,256]{2,1,0:T(8,128)} fusion(f32[32,128,256]{2,1,0:T(8,128)} %get-tuple-element.237, s32[32]{0:T(128)S(1)} %get-tuple-element.219, f32[32,128,256]{2,1,0:T(8,128)} %fusion.37), kind=kCustom, calls=%fused_computation.4.clone.1 | custom fusion | flops 1048576 | bytes 12583040 | tf_op jit(solution)/shard_map/while/body/eval_jaxpr/scatter-add | solution.py:58
  318.6 0.7 gather_fusion
  319.3 3.9 fusion.37
  323.2 9.5 %scatter_fusion = f32[32,128,256]{2,1,0:T(8,128)} fusion(f32[32,128,256]{2,1,0:T(8,128)} %get-tuple-element.237, s32[32]{0:T(128)S(1)} %get-tuple-element.219, f32[32,128,256]{2,1,0:T(8,128)} %fusion.37), kind=kCustom, calls=%fused_computation.4.clone.1 | custom fusion | flops 1048576 | bytes 12583040 | tf_op jit(solution)/shard_map/while/body/eval_jaxpr/scatter-add | solution.py:58
  333.4 3.9 fusion.37
  337.3 9.6 %scatter_fusion = f32[32,128,256]{2,1,0:T(8,128)} fusion(f32[32,128,256]{2,1,0:T(8,128)} %get-tuple-element.237, s32[32]{0:T(128)S(1)} %get-tuple-element.219, f32[32,128,256]{2,1,0:T(8,128)} %fusion.37), kind=kCustom, calls=%fused_computation.4.clone.1 | custom fusion | flops 1048576 | bytes 12583040 | tf_op jit(solution)/shard_map/while/body/eval_jaxpr/scatter-add | solution.py:58
  347.6 3.9 fusion.37
  351.5 9.7 %scatter_fusion = f32[32,128,256]{2,1,0:T(8,128)} fusion(f32[32,128,256]{2,1,0:T(8,128)} %get-tuple-element.237, s32[32]{0:T(128)S(1)} %get-tuple-element.219, f32[32,128,256]{2,1,0:T(8,128)} %fusion.37), kind=kCustom, calls=%fused_computation.4.clone.1 | custom fusion | flops 1048576 | bytes 12583040 | tf_op jit(solution)/shard_map/while/body/eval_jaxpr/scatter-add | solution.py:58
  361.9 3.9 fusion.37
  365.8 9.9 %scatter_fusion = f32[32,128,256]{2,1,0:T(8,128)} fusion(f32[32,128,256]{2,1,0:T(8,128)} %get-tuple-element.237, s32[32]{0:T(128)S(1)} %get-tuple-element.219, f32[32,128,256]{2,1,0:T(8,128)} %fusion.37), kind=kCustom, calls=%fused_computation.4.clone.1 | custom fusion | flops 1048576 | bytes 12583040 | tf_op jit(solution)/shard_map/while/body/eval_jaxpr/scatter-add | solution.py:58
  375.7 77.3 %all-reduce.1 = bf16[32,128,256]{2,1,0:T(8,128)(2,1)} all-reduce(f32[32,128,256]{2,1,0:T(8,128)} %get-tuple-element.66), channel_id=1, replica_groups=mesh['grp'=2,'reg'=4,'dev'=4] {'reg'}, use_global_device_ids=true, to_apply=%region_6.7 | all-reduce | flops 1048576 | bytes 6291456 | tf_op jit(solution)/shard_map/psum | solution.py:64
  453.2 118.4 %while.21 = (s32[]{:T(128)}, f32[16,128,256]{2,1,0:T(8,128)S(1)}, s32[8,32]{1,0:T(8,128)S(1)}, bf16[8,32,128,128]{3,2,1,0:T(8,128)(2,1)}, s32[8,32]{1,0:T(8,128)S(1)}, /*index=5*/bf16[32,128,256]{2,1,0:T(8,128)(2,1)}, s32[]{:T(128)}) while((s32[]{:T(128)}, f32[16,128,256]{2,1,0:T(8,128)S(1)}, s32[8,32]{1,0:T(8,128)S(1)}, ...), condition=%wide.region_9.10_spmd, body=%wide.region_7.9_spmd.sunk | while | flops 269485248 | bytes 24122832 | solution.py:73
  453.3 3.6 gather_fusion.1
  456.9 4.7 fusion.41
  461.6 6.5 %scatter_fusion.1 = f32[16,128,256]{2,1,0:T(8,128)S(1)} fusion(f32[16,128,256]{2,1,0:T(8,128)S(1)} %get-tuple-element.258, s32[32]{0:T(128)S(1)} %get-tuple-element.227, f32[32,128,256]{2,1,0:T(8,128)} %fusion.41), kind=kCustom, calls=%fused_computation.5.clone.1 | custom fusion | flops 1048576 | bytes 12583040 | tf_op jit(solution)/shard_map/while/body/eval_jaxpr/scatter-add | solution.py:70
  468.1 3.6 gather_fusion.1
  471.7 4.7 fusion.41
  476.3 6.5 %scatter_fusion.1 = f32[16,128,256]{2,1,0:T(8,128)S(1)} fusion(f32[16,128,256]{2,1,0:T(8,128)S(1)} %get-tuple-element.258, s32[32]{0:T(128)S(1)} %get-tuple-element.227, f32[32,128,256]{2,1,0:T(8,128)} %fusion.41), kind=kCustom, calls=%fused_computation.5.clone.1 | custom fusion | flops 1048576 | bytes 12583040 | tf_op jit(solution)/shard_map/while/body/eval_jaxpr/scatter-add | solution.py:70
  482.9 3.6 gather_fusion.1
  486.5 4.7 fusion.41
  491.2 6.5 %scatter_fusion.1 = f32[16,128,256]{2,1,0:T(8,128)S(1)} fusion(f32[16,128,256]{2,1,0:T(8,128)S(1)} %get-tuple-element.258, s32[32]{0:T(128)S(1)} %get-tuple-element.227, f32[32,128,256]{2,1,0:T(8,128)} %fusion.41), kind=kCustom, calls=%fused_computation.5.clone.1 | custom fusion | flops 1048576 | bytes 12583040 | tf_op jit(solution)/shard_map/while/body/eval_jaxpr/scatter-add | solution.py:70
  497.7 3.6 gather_fusion.1
  501.3 4.7 fusion.41
  506.0 6.5 %scatter_fusion.1 = f32[16,128,256]{2,1,0:T(8,128)S(1)} fusion(f32[16,128,256]{2,1,0:T(8,128)S(1)} %get-tuple-element.258, s32[32]{0:T(128)S(1)} %get-tuple-element.227, f32[32,128,256]{2,1,0:T(8,128)} %fusion.41), kind=kCustom, calls=%fused_computation.5.clone.1 | custom fusion | flops 1048576 | bytes 12583040 | tf_op jit(solution)/shard_map/while/body/eval_jaxpr/scatter-add | solution.py:70
  512.5 3.6 gather_fusion.1
  516.1 4.7 fusion.41
  520.8 6.4 %scatter_fusion.1 = f32[16,128,256]{2,1,0:T(8,128)S(1)} fusion(f32[16,128,256]{2,1,0:T(8,128)S(1)} %get-tuple-element.258, s32[32]{0:T(128)S(1)} %get-tuple-element.227, f32[32,128,256]{2,1,0:T(8,128)} %fusion.41), kind=kCustom, calls=%fused_computation.5.clone.1 | custom fusion | flops 1048576 | bytes 12583040 | tf_op jit(solution)/shard_map/while/body/eval_jaxpr/scatter-add | solution.py:70
  527.3 3.6 gather_fusion.1
  530.9 4.7 fusion.41
  535.6 6.5 %scatter_fusion.1 = f32[16,128,256]{2,1,0:T(8,128)S(1)} fusion(f32[16,128,256]{2,1,0:T(8,128)S(1)} %get-tuple-element.258, s32[32]{0:T(128)S(1)} %get-tuple-element.227, f32[32,128,256]{2,1,0:T(8,128)} %fusion.41), kind=kCustom, calls=%fused_computation.5.clone.1 | custom fusion | flops 1048576 | bytes 12583040 | tf_op jit(solution)/shard_map/while/body/eval_jaxpr/scatter-add | solution.py:70
  542.1 3.6 gather_fusion.1
  545.7 4.7 fusion.41
  550.4 6.5 %scatter_fusion.1 = f32[16,128,256]{2,1,0:T(8,128)S(1)} fusion(f32[16,128,256]{2,1,0:T(8,128)S(1)} %get-tuple-element.258, s32[32]{0:T(128)S(1)} %get-tuple-element.227, f32[32,128,256]{2,1,0:T(8,128)} %fusion.41), kind=kCustom, calls=%fused_computation.5.clone.1 | custom fusion | flops 1048576 | bytes 12583040 | tf_op jit(solution)/shard_map/while/body/eval_jaxpr/scatter-add | solution.py:70
  556.9 3.6 gather_fusion.1
  560.5 4.7 fusion.41
  565.2 6.4 %scatter_fusion.1 = f32[16,128,256]{2,1,0:T(8,128)S(1)} fusion(f32[16,128,256]{2,1,0:T(8,128)S(1)} %get-tuple-element.258, s32[32]{0:T(128)S(1)} %get-tuple-element.227, f32[32,128,256]{2,1,0:T(8,128)} %fusion.41), kind=kCustom, calls=%fused_computation.5.clone.1 | custom fusion | flops 1048576 | bytes 12583040 | tf_op jit(solution)/shard_map/while/body/eval_jaxpr/scatter-add | solution.py:70
  571.6 1.1 convert_element_type.21
  572.8 26.5 %reduce-scatter.2.cloned.1.call-done = bf16[4,128,256]{2,1,0:T(8,128)(2,1)} async-done(((bf16[16,128,256]{2,1,0:T(8,128)(2,1)}), bf16[4,128,256]{2,1,0:T(8,128)(2,1)}) %reduce-scatter.2.cloned.1.call-update) | async-done | bytes 262160 | tf_op jit(solution)/shard_map/reduce_scatter | solution.py:77
  599.3 1.8 bitcast_convert_fusion
  (56 shorter events, 3.2 us)
Async XLA Ops:
  7.2 0.8 copy-start
  18.9 33.4 %all-to-all-start = ((bf16[16,16,2]{1,2,0:T(2,128)(2,1)}), bf16[16,16,2]{1,2,0:T(2,128)(2,1)S(1)}, u32[]{:S(2)}, u32[]{:S(2)}) async-start(bf16[16,16,2]{1,2,0:T(2,128)(2,1)} %copy.26), calls=%async_computation | async-start | bytes 16384 | tf_op jit(solution)/shard_map/all_to_all | solution.py:41
  52.3 207.2 %all-to-all-start.1 = ((bf16[16,16,128,128]{3,2,1,0:T(8,128)(2,1)}), bf16[16,16,128,128]{3,2,1,0:T(8,128)(2,1)}, u32[]{:S(2)}, u32[]{:S(2)}) async-start(bf16[16,16,128,128]{3,2,1,0:T(8,128)(2,1)} %scatter_fusion.3), calls=%async_computation.1 | async-start | bytes 16777216 | tf_op jit(solution)/shard_map/all_to_all | solution.py:40
  58.4 75.7 %all-gather.2.cloned.1.call-start = ((), (), s32[]{:S(2)}) async-start(), calls=%async_computation.3 | async-start | bytes 1310720 | tf_op jit(solution)/shard_map/all_gather | solution.py:50
  59.2 540.1 %reduce-scatter.2.cloned.1.call-start = ((), (), s32[]{:S(2)}) async-start(), calls=%async_computation.4 | async-start | bytes 1310720 | tf_op jit(solution)/shard_map/reduce_scatter | solution.py:77
  134.1 128.0 %copy-start.1 = (bf16[2048,256]{1,0:T(8,128)(2,1)S(1)}, bf16[2048,256]{1,0:T(8,128)(2,1)}, u32[]{:S(2)}) copy-start(bf16[2048,256]{1,0:T(8,128)(2,1)} %all-gather.2.cloned.1.call-done) | copy-start | bytes 3145732
Sparse Core Ops, SparseCore 0:
  60.8 73.2 all-gather.1
  572.9 26.3 reduce-scatter.1
where the time goes:
time: 609 us; the launch traced here: 608 us
  waiting for transfers between devices  227 us (37%)
  other arithmetic  133 us (22%)
  blocking collectives  77.3 us (13%)
  local copies, waits for them, and re-layouts  74.2 us (12%)
  matrix products  68.5 us (11%)
  between operations  14.1 us (2%)
  starting transfers between devices  13.5 us (2%)
    all_to_all x1, waiting for transfers between devices, local(): lax.all_to_all(send_blocks, ('reg', 'dev'), split_axis=0, concat_axis=0,...  126 us
    psum x1, blocking collectives, local(): receptor_image = lax.psum(receptor_part, 'reg').astype(jnp.bfloat16)  77.3 us
    scatter-add x8, other arithmetic, forward_step(): return (running.at[rec_slot].add(terms), None)  76.8 us
    all_gather x1, waiting for transfers between devices, local(): lax.all_gather(probe_matrix, 'dev', axis=0, tiled=True)  74.6 us
    scatter-add x8, other arithmetic, backward_step(): return (running.at[src_slot].add(terms), None)  51.7 us
    dot_general x8, matrix products, backward_step(): jnp.einsum('gji,gjk->gik', pieces, taken, preferred_element_type=jnp.floa...  37.2 us
    dot_general x8, matrix products, forward_step(): jnp.einsum('gij,gjk->gik', pieces, taken, preferred_element_type=jnp.floa...  31.3 us
    gather x8, local copies, waits for them, and re-layouts, backward_step(): taken = receptor_image[rec_slot]  29.1 us
  transfers between devices with their start and end apart: 4, of which 3 were waited for; matrix products, arithmetic and copies ran while one was open for 4% of the time, Pallas kernels for 0%

commit v1 on v0

v1 whole, which is shorter than its diff:
```python
import functools

import jax
import jax.numpy as jnp
from jax import lax
from jax.experimental import pallas as pl
from jax.experimental.pallas import tpu as pltpu
from jax.sharding import PartitionSpec as P

MESH = pl.DeviceIdType.MESH
ANY = pl.BlockSpec(memory_space=pl.ANY)
VMEM_LIMIT = 60 * 2**20
SPLIT = 2


class Ring:
    def __init__(self, reg, dev):
        self.reg, self.dev = reg, dev
        self.chips = reg // 2 * dev
        self.half = self.chips // 2
        r, z = lax.axis_index("reg"), lax.axis_index("dev")
        x, self.core = r // 2, r % 2
        self.at = x * dev + z + (x % 2) * (dev - 1 - 2 * z)
        self.sign = 1 - 2 * self.core

    def place(self, steps):
        at = lax.rem(self.at + steps + 2 * self.chips, self.chips)
        x, z = at // self.dev, at % self.dev
        return x, z + (x % 2) * (self.dev - 1 - 2 * z)

    def device(self, steps, other=0):
        x, z = self.place(steps)
        return {"reg": 2 * x + (self.core if not other else 1 - self.core), "dev": z}

    def chunk(self, by_dev, steps, other=0):
        x, z = self.place(steps)
        r = 2 * x + (self.core if not other else 1 - self.core)
        return z * self.reg + r if by_dev else r * self.dev + z

    def partners(self):
        return self.device(self.sign), self.device(-self.sign), self.device(0, 1)

    def barrier(self):
        barrier = pltpu.get_barrier_semaphore()
        for who in self.partners():
            pl.semaphore_signal(barrier, inc=1, device_id=who, device_id_type=MESH)
        pl.semaphore_wait(barrier, 3)


def remote(src, dst, send, recv, who):
    return pltpu.make_async_remote_copy(
        src_ref=src, dst_ref=dst, send_sem=send, recv_sem=recv, device_id=who, device_id_type=MESH
    )


def order_of_use(half):
    order = []
    for step in range(half):
        order.append(("a", step))
        if step < half - 1:
            order.append(("b", step))
    return order + [("own", 0)]


def scatter_steps(half, way, step):
    return {"a": half - step, "b": -(half - 1 - step), "own": 0}[way]


def add_rows(out, refs, rows):
    start, size = rows
    tile = min(size, 64)

    @pl.loop(0, size // tile)
    def _(i):
        where = pl.ds(pl.multiple_of(start + i * tile, tile), tile)
        total = refs[0][where, :].astype(jnp.float32)
        for ref in refs[1:]:
            total += ref[where, :].astype(jnp.float32)
        out[where, :] = total.astype(out.dtype)


def reduce_scatter(ring, by_dev, part, out, after, scratch):
    mine, theirs, from_a, from_b, local_sem, pair_send, pair_recv, a_send, a_recv, b_send, b_recv = scratch
    half = ring.half
    size = part.shape[1] // SPLIT
    order = order_of_use(half)
    to_a, to_b, sibling = ring.partners()
    copies, pairs = [], []
    for j, (way, step) in enumerate(order):
        steps = scatter_steps(half, way, step)
        pair = remote(
            part.at[ring.chunk(by_dev, -ring.sign * steps, 1)],
            theirs.at[j], pair_send.at[j], pair_recv.at[j], sibling,
        )
        pair.start()
        pairs.append(pair)
        copy = pltpu.make_async_copy(
            part.at[ring.chunk(by_dev, ring.sign * steps)], mine.at[j], local_sem.at[j]
        )
        copy.start()
        copies.append(copy)
    sent = {}
    for j, (way, step) in enumerate(order):
        copies[j].wait()
        pairs[j].wait_recv()
        for h in range(SPLIT):
            rows = pl.ds(h * size, size)
            refs = [mine.at[j], theirs.at[j]]
            if way == "own":
                sent["a", half - 1, h].wait_recv()
                refs.append(from_a.at[half - 1])
                if half > 1:
                    sent["b", half - 2, h].wait_recv()
                    refs.append(from_b.at[half - 2])
                add_rows(out, refs, (h * size, size))
                after(h)
                continue
            landing, send, recv, who = (
                (from_a, a_send, a_recv, to_a) if way == "a" else (from_b, b_send, b_recv, to_b)
            )
            if step:
                sent[way, step - 1, h].wait_recv()
                refs.append(landing.at[step - 1])
            add_rows(mine.at[j], refs, (h * size, size))
            copy = remote(
                mine.at[j, rows], landing.at[step, rows],
                send.at[step * SPLIT + h], recv.at[step * SPLIT + h], who,
            )
            copy.start()
            sent[way, step, h] = copy
    for copy in sent.values():
        copy.wait_send()
    for pair in pairs:
        pair.wait_send()


def scatter_scratch(chips, rows, columns):
    half = chips // 2
    dma = pltpu.SemaphoreType.DMA
    return [
        pltpu.VMEM((chips, rows, columns), jnp.bfloat16),
        pltpu.VMEM((chips, rows, columns), jnp.bfloat16),
        pltpu.VMEM((half, rows, columns), jnp.bfloat16),
        pltpu.VMEM((max(half - 1, 1), rows, columns), jnp.bfloat16),
        dma((chips,)), dma((chips,)), dma((chips,)),
        dma((half * SPLIT,)), dma((half * SPLIT,)), dma((half * SPLIT,)), dma((half * SPLIT,)),
    ]


class Gather:
    def __init__(self, ring, by_dev, own, full, scratch):
        self.ring, self.by_dev, self.own, self.full = ring, by_dev, own, full
        self.local_sem, self.sems = scratch[0], scratch[1:]
        self.size = own.shape[0] // SPLIT
        self.sent, self.started = {}, []

    def piece(self, steps, h):
        return self.full.at[self.ring.chunk(self.by_dev, steps), pl.ds(h * self.size, self.size)]

    def send(self, way, step, h):
        ring = self.ring
        steps = {"a": -step, "b": step, "p": -step, "q": step}[way]
        steps = ring.sign * steps
        dst = self.piece(steps, h)
        src = self.own.at[pl.ds(h * self.size, self.size)] if step == 0 else dst
        i = "abpq".index(way)
        who = ring.partners()[min(i, 2)]
        index = step * SPLIT + h
        copy = remote(src, dst, self.sems[2 * i].at[index], self.sems[2 * i + 1].at[index], who)
        copy.start()
        self.sent[way, step, h] = copy

    def start(self, h):
        copy = pltpu.make_async_copy(
            self.own.at[pl.ds(h * self.size, self.size)], self.piece(0, h), self.local_sem.at[h]
        )
        copy.start()
        self.started.append(copy)
        self.send("a", 0, h)
        if self.ring.half > 1:
            self.send("b", 0, h)
        self.send("p", 0, h)

    def finish(self):
        half = self.ring.half
        for step in range(1, half + 1):
            for h in range(SPLIT):
                self.sent["a", step - 1, h].wait_recv()
                if step < half:
                    self.send("a", step, h)
                self.send("p", step, h)
                if step < half:
                    self.sent["b", step - 1, h].wait_recv()
                    if step < half - 1:
                        self.send("b", step, h)
                    self.send("q", step, h)
        for copy in self.started:
            copy.wait()
        for (way, step, h), copy in self.sent.items():
            copy.wait_send()
            if way in "pq":
                copy.wait_recv()


def gather_scratch(chips):
    dma = pltpu.SemaphoreType.DMA
    return [dma((SPLIT,))] + [dma(((chips // 2 + 1) * SPLIT,))] * 8


def gather_kernel(reg, dev, own, full, *scratch):
    ring = Ring(reg, dev)
    ring.barrier()
    gather = Gather(ring, False, own, full, scratch)
    for h in range(SPLIT):
        gather.start(h)
    gather.finish()


def image_kernel(reg, dev, part, full, shard, *scratch):
    ring = Ring(reg, dev)
    ring.barrier()
    gather = Gather(ring, True, shard, full, scratch[11:])
    reduce_scatter(ring, True, part, shard, gather.start, scratch[:11])
    gather.finish()


def scatter_kernel(reg, dev, part, out, *scratch):
    ring = Ring(reg, dev)
    ring.barrier()
    reduce_scatter(ring, False, part, out, lambda h: None, scratch)


def remote_params(collective_id):
    return pltpu.CompilerParams(
        collective_id=collective_id, has_side_effects=True, vmem_limit_bytes=VMEM_LIMIT
    )


def multiply_kernel(transposed, order, keep, pos, take, blocks, table, out):
    count = blocks.shape[0]
    zero = jnp.zeros(out.shape[1:], out.dtype)

    @pl.loop(0, out.shape[0])
    def _(i):
        out[i] = zero

    contract = ((0,), (0,)) if transposed else ((1,), (0,))

    def step(i, total):
        term = lax.dot_general(
            blocks[order[i]], table[take[i]], (contract, ((), ())),
            preferred_element_type=jnp.float32,
        )
        total = jnp.where(keep[i] == 1, total, 0.0) + term
        out[pos[i]] = total.astype(out.dtype)
        return total

    lax.fori_loop(0, count, step, jnp.zeros(out.shape[1:], jnp.float32), unroll=4)


def multiply(transposed, plan, blocks, table, positions):
    count, cells, _ = blocks.shape
    rows, _, columns = table.shape
    held = (rows + positions) * cells * columns * 2
    pieces = 1 if held <= 40 * 2**20 else 2
    width = columns // pieces
    once = pl.Buffered(1)
    return pl.pallas_call(
        functools.partial(multiply_kernel, transposed),
        out_shape=jax.ShapeDtypeStruct((positions, cells, columns), jnp.bfloat16),
        grid_spec=pltpu.PrefetchScalarGridSpec(
            num_scalar_prefetch=4,
            grid=(pieces,),
            in_specs=[
                pl.BlockSpec((count, cells, cells), lambda i, *_: (0, 0, 0), pipeline_mode=once),
                pl.BlockSpec((rows, cells, width), lambda i, *_: (0, 0, i), pipeline_mode=once),
            ],
            out_specs=pl.BlockSpec((positions, cells, width), lambda i, *_: (0, 0, i), pipeline_mode=once),
        ),
        compiler_params=pltpu.CompilerParams(vmem_limit_bytes=VMEM_LIMIT),
    )(*plan, blocks, table)


def look_up(place, index):
    hit = index[:, None] == jnp.arange(place.shape[0], dtype=jnp.int32)[None, :]
    return jnp.sum(jnp.where(hit, place[None, :], 0), axis=1)


def sorted_plan(pos, take):
    count = pos.shape[0]
    number = jnp.arange(count, dtype=jnp.int32)
    key = pos * count + number
    rank = jnp.sum((key[None, :] < key[:, None]).astype(jnp.int32), axis=1)
    hit = rank[None, :] == number[:, None]
    pick = lambda values: jnp.sum(jnp.where(hit, values[None, :], 0), axis=1)
    pos_sorted = pick(pos)
    before = jnp.concatenate([jnp.full((1,), -1, jnp.int32), pos_sorted[:-1]])
    return pick(number), (pos_sorted == before).astype(jnp.int32), pos_sorted, pick(take)


def local(footprints, block_coords, receptor_place, source_place, probe_matrix):
    cells = footprints.shape[1]
    columns = probe_matrix.shape[1]
    reg, dev = lax.axis_size("reg"), lax.axis_size("dev")
    chips, devices = reg // 2 * dev, reg * dev
    receptors = receptor_place.shape[0]
    sources = probe_matrix.shape[0] * devices // cells
    bf16 = jnp.bfloat16

    pos_rec = look_up(receptor_place, block_coords[:, 0])
    pos_src = look_up(source_place, block_coords[:, 1])
    forward_plan = sorted_plan(pos_rec, pos_src)
    backward_plan = sorted_plan(pos_src, pos_rec)

    probe_rows = probe_matrix.shape[0]
    probe = pl.pallas_call(
        functools.partial(gather_kernel, reg, dev),
        out_shape=jax.ShapeDtypeStruct((devices, probe_rows, columns), bf16),
        in_specs=[ANY], out_specs=ANY,
        scratch_shapes=gather_scratch(chips),
        compiler_params=remote_params(1),
    )(probe_matrix)

    receptor_part = multiply(False, forward_plan, footprints, probe.reshape(sources, cells, columns), receptors)

    image_rows = receptors * cells // devices
    image = pl.pallas_call(
        functools.partial(image_kernel, reg, dev),
        out_shape=jax.ShapeDtypeStruct((devices, image_rows, columns), bf16),
        in_specs=[ANY], out_specs=ANY,
        scratch_shapes=[pltpu.VMEM((image_rows, columns), bf16)]
        + scatter_scratch(chips, image_rows, columns) + gather_scratch(chips),
        compiler_params=remote_params(2),
    )(receptor_part.reshape(devices, image_rows, columns))
    receptor_image = lax.dynamic_slice_in_dim(image, lax.axis_index("dev") * reg, reg, 0)

    source_part = multiply(True, backward_plan, footprints, image.reshape(receptors, cells, columns), sources)

    source_image = pl.pallas_call(
        functools.partial(scatter_kernel, reg, dev),
        out_shape=jax.ShapeDtypeStruct((probe_rows, columns), jnp.float32),
        in_specs=[ANY], out_specs=pl.BlockSpec(memory_space=pltpu.VMEM),
        scratch_shapes=scatter_scratch(chips, probe_rows, columns),
        compiler_params=remote_params(3),
    )(source_part.reshape(devices, probe_rows, columns))
    return receptor_image.reshape(reg * image_rows, columns), source_image


def solution(mesh):
    return jax.shard_map(
        local,
        mesh=mesh,
        in_specs=(
            P(("grp", "reg", "dev"), None, None),
            P(("grp", "reg", "dev"), None),
            P("grp"),
            P("grp"),
            P(("grp", "reg", "dev"), None),
        ),
        out_specs=(P(("grp", "dev"), None), P(("grp", "reg", "dev"), None)),
        check_vma=False,
    )
```

time: 609 us -> 184 us (0.30)
  waiting for transfers between devices: 227 us -> 0 us
  Pallas kernels: 0 us -> 175 us
  other arithmetic: 133 us -> 3.33 us
  blocking collectives: 77.3 us -> 0 us
  local copies, waits for them, and re-layouts: 74.2 us -> 4.67 us
  matrix products: 68.5 us -> 0 us
  starting transfers between devices: 13.5 us -> 0 us
  between operations: 14.1 us -> 0.7 us
    pallas_call x0 -> x5, Pallas kernels: none -> 175 us  [the longest x1 87.1 us: local(): pl.pallas_call(functools.partial(image_kernel, reg, dev), out_shape=jax.S...]
    scatter-add x16 -> x0, other arithmetic: 128 us -> none  [the longest x8 76.8 us: forward_step(): return (running.at[rec_slot].add(terms), None)]
    all_to_all x2 -> x0, waiting for transfers between devices: 126 us -> none  [the longest x1 126 us: local(): lax.all_to_all(send_blocks, ('reg', 'dev'), split_axis=0, concat_axis=0,...]
    psum x1 -> x0, blocking collectives: 77.3 us -> none  [local(): receptor_image = lax.psum(receptor_part, 'reg').astype(jnp.bfloat16)]
    all_gather x1 -> x0, waiting for transfers between devices: 74.6 us -> none  [local(): lax.all_gather(probe_matrix, 'dev', axis=0, tiled=True)]
    dot_general x16 -> x0, matrix products: 68.5 us -> none  [the longest x8 37.2 us: backward_step(): jnp.einsum('gji,gjk->gik', pieces, taken, preferred_element_type=jnp.floa...]
    gather x18 -> x0, local copies, waits for them, and re-layouts: 37.3 us -> none  [the longest x8 29.1 us: backward_step(): taken = receptor_image[rec_slot]]
    scatter x3 -> x0, local copies, waits for them, and re-layouts: 28.4 us -> none  [the longest x1 20.7 us: local(): send_blocks = jnp.zeros((owners, capacity, cells, cells), jnp.bfloat16).a...]
  transfers between devices with their start and end apart: 4 -> 0, of which waited for: 3 -> 0; matrix products, arithmetic and copies ran while one was open for 4% -> 0% of each run, Pallas kernels for 0% -> 0%
where the time goes in v1:
time: 184 us; the launch traced here: 183 us
  Pallas kernels  175 us (95%)
  local copies, waits for them, and re-layouts  4.67 us (3%)
  other arithmetic  3.33 us (2%)
    pallas_call x1, Pallas kernels, local(): pl.pallas_call(functools.partial(image_kernel, reg, dev), out_shape=jax.S...  87.1 us
    pallas_call x2, Pallas kernels, multiply(): pl.pallas_call(functools.partial(multiply_kernel, transposed), out_shape=...  31.3 us
    pallas_call x1, Pallas kernels, local(): pl.pallas_call(functools.partial(gather_kernel, reg, dev), out_shape=jax....  29.3 us
    pallas_call x1, Pallas kernels, local(): pl.pallas_call(functools.partial(scatter_kernel, reg, dev), out_shape=jax...  27 us

profile of v1, /device:TPU:0, one launch (start us, length us, event | category | flops | bytes accessed | tf_op | source)
XLA Modules:
  0.0 183.4 jit_solution(6108621817467487529)
XLA Ops:
  0.6 0.8 slice_bitcast_fusion.1
  1.4 0.7 select_reduce_fusion.7
  2.1 0.2 convert_reduce_fusion
  2.3 0.8 select_reduce_fusion.6
  3.2 0.2 convert_reduce_fusion.1
  3.4 0.7 select_reduce_fusion
  4.1 0.0 copy-start.2
  4.1 0.0 copy-start.1
  4.1 0.7 compare_convert_fusion
  4.7 29.3 %shard_map.68 = bf16[16,512,256]{2,1,0:T(8,128)(2,1)} custom-call(bf16[512,256]{1,0:T(8,128)(2,1)} %own.1), custom_call_target="tpu_custom_call" | custom-call | tf_op jit(solution)/shard_map/pallas_call | solution.py:316
  34.1 0.0 copy-done.2
  34.1 15.2 %shard_map.69 = bf16[128,128,256]{2,1,0:T(8,128)(2,1)} custom-call(s32[128]{0:T(128)} %get-tuple-element.6.order, s32[128]{0:T(128)} %get-tuple-element.11.keep, s32[128]{0:T(128)} %copy-done.2, s32[128]{0:T(128)} %get-tuple-element.4.take, bf16[128,128,128]{2,1,0:T(8,128)(2,1)} %blocks.3, bf16[64,128,256]{2,1,0:T(8,128)(2,1)} %bitcast.13), custom_call_target="tpu_custom_call" | custom-call | tf_op jit(solution)/shard_map/pallas_call | solution.py:268
  49.3 0.0 copy-done.1
  49.4 87.1 %shard_map.70 = bf16[16,1024,256]{2,1,0:T(8,128)(2,1)} custom-call(bf16[16,1024,256]{2,1,0:T(8,128)(2,1)} %bitcast.12), custom_call_target="tpu_custom_call" | custom-call | tf_op jit(solution)/shard_map/pallas_call | solution.py:327
  136.5 16.0 %shard_map.71 = bf16[64,128,256]{2,1,0:T(8,128)(2,1)} custom-call(s32[128]{0:T(128)} %get-tuple-element.7.order, s32[128]{0:T(128)} %get-tuple-element.10.keep, s32[128]{0:T(128)} %copy-done.1, s32[128]{0:T(128)} %get-tuple-element.2.take, bf16[128,128,128]{2,1,0:T(8,128)(2,1)} %blocks.3, bf16[128,128,256]{2,1,0:T(8,128)(2,1)} %bitcast.11), custom_call_target="tpu_custom_call" | custom-call | tf_op jit(solution)/shard_map/pallas_call | solution.py:268
  152.5 27.0 %shard_map.72 = f32[512,256]{1,0:T(8,128)} custom-call(bf16[16,512,256]{2,1,0:T(8,128)(2,1)} %bitcast.14), custom_call_target="tpu_custom_call" | custom-call | tf_op jit(solution)/shard_map/pallas_call | solution.py:339
  179.5 0.0 copy-start
  179.5 3.1 %constant_dynamic-slice_fusion = bf16[4,1024,256]{2,1,0:T(8,128)(2,1)} fusion(bf16[16,1024,256]{2,1,0:T(8,128)(2,1)} %shard_map.70, s32[]{:T(128)S(6)} %select_n.34), kind=kLoop, calls=%fused_computation.22 | loop fusion | bytes 4194308 | tf_op jit(solution)/shard_map/dynamic_slice | solution.py:335
  182.6 0.0 copy-done
  182.6 0.8 copy.8
  (2 shorter events, 0.0 us)
Async XLA Ops:
  4.1 30.0 %copy-start.2 = (s32[128]{0:T(128)}, s32[128]{0:T(128)S(1)}, u32[]{:S(2)}) copy-start(s32[128]{0:T(128)S(1)} %get-tuple-element.3.pos) | copy-start | bytes 1540
  4.1 45.3 %copy-start.1 = (s32[128]{0:T(128)}, s32[128]{0:T(128)S(1)}, u32[]{:S(2)}) copy-start(s32[128]{0:T(128)S(1)} %get-tuple-element.5.pos) | copy-start | bytes 1540
  179.5 3.1 %copy-start = (f32[512,256]{1,0:T(8,128)S(1)}, f32[512,256]{1,0:T(8,128)}, u32[]{:S(2)}) copy-start(f32[512,256]{1,0:T(8,128)} %shard_map.72) | copy-start | bytes 1572868

commit v2 on v1

--- a/solution.py
+++ b/solution.py
@@ -11,6 +11,8 @@
 ANY = pl.BlockSpec(memory_space=pl.ANY)
 VMEM_LIMIT = 60 * 2**20
 SPLIT = 2
+SLICES = 16
+AHEAD = 3
 
 
 class Ring:
@@ -281,6 +283,335 @@
     )(*plan, blocks, table)
 
 
+class HalfGather:
+    def __init__(self, ring, by_dev, full, scratch):
+        self.ring, self.by_dev, self.full, self.sems = ring, by_dev, full, scratch
+        self.blocks = full.shape[0] // (2 * ring.chips)
+        self.size = self.blocks // SPLIT
+        self.sent = {}
+
+    def send(self, way, step, h):
+        ring = self.ring
+        steps = ring.sign * {"a": -step, "b": step, "p": -step, "q": step}[way]
+        first = ring.chunk(self.by_dev, steps) * self.blocks + h * self.size
+        piece = self.full.at[pl.ds(first, self.size)]
+        i = "abpq".index(way)
+        index = step * SPLIT + h
+        copy = remote(
+            piece, piece, self.sems[2 * i].at[index], self.sems[2 * i + 1].at[index],
+            ring.partners()[min(i, 2)],
+        )
+        copy.start()
+        self.sent[way, step, h] = copy
+
+    def start(self, h):
+        self.send("a", 0, h)
+        if self.ring.half > 1:
+            self.send("b", 0, h)
+        self.send("p", 0, h)
+
+    def step(self, step, work):
+        half = self.ring.half
+        for h in range(SPLIT):
+            work()
+            self.sent["a", step - 1, h].wait_recv()
+            if step < half:
+                self.send("a", step, h)
+            self.send("p", step, h)
+            if step < half:
+                work()
+                self.sent["b", step - 1, h].wait_recv()
+                if step < half - 1:
+                    self.send("b", step, h)
+                self.send("q", step, h)
+
+    def advance(self, work):
+        for step in range(1, self.ring.half):
+            self.step(step, work)
+
+    def tail(self):
+        self.step(self.ring.half, lambda: None)
+        for (way, step, h), copy in self.sent.items():
+            if way in "pq":
+                copy.wait_recv()
+
+    def drain(self):
+        for copy in self.sent.values():
+            copy.wait_send()
+
+
+class HalfScatter:
+    def __init__(self, ring, by_dev, part, scratch):
+        self.ring, self.by_dev, self.part = ring, by_dev, part
+        self.theirs, self.from_a, self.from_b = scratch[:3]
+        self.pair_send, self.pair_recv, self.a_send, self.a_recv, self.b_send, self.b_recv = scratch[3:]
+        self.order = order_of_use(ring.half)
+        self.blocks = part.shape[0] // (2 * ring.chips)
+        self.size = self.blocks // SPLIT
+        self.pairs, self.sent = [], {}
+
+    def pair(self):
+        j = len(self.pairs)
+        if j == len(self.order):
+            return
+        ring = self.ring
+        steps = scatter_steps(ring.half, *self.order[j])
+        first = ring.chunk(self.by_dev, -ring.sign * steps, 1) * self.blocks
+        copy = remote(
+            self.part.at[pl.ds(first, self.blocks)], self.theirs.at[pl.ds(j * self.blocks, self.blocks)],
+            self.pair_send.at[j], self.pair_recv.at[j], ring.device(0, 1),
+        )
+        copy.start()
+        self.pairs.append(copy)
+
+    def chunk(self, j, work, store, after):
+        ring, half = self.ring, self.ring.half
+        way, step = self.order[j]
+        work()
+        self.pairs[j].wait_recv()
+        self.pair()
+        to_a, to_b, _ = ring.partners()
+        for h in range(SPLIT):
+            first = ring.chunk(self.by_dev, ring.sign * scatter_steps(half, way, step)) * self.blocks
+            mine = self.part.at[pl.ds(first + h * self.size, self.size)]
+            refs = [mine, self.theirs.at[pl.ds(j * self.blocks + h * self.size, self.size)]]
+            before = [("a", half - 1), ("b", half - 2)] if way == "own" else [(way, step - 1)]
+            for w, s in before:
+                if s >= 0:
+                    work()
+                    self.sent[w, s, h].wait_recv()
+                    landing = self.from_a if w == "a" else self.from_b
+                    refs.append(landing.at[pl.ds(s * self.blocks + h * self.size, self.size)])
+            put = (lambda i, v: store(h * self.size + i, v)) if way == "own" else None
+
+            @pl.loop(0, self.size)
+            def _(i):
+                total = refs[0][i].astype(jnp.float32)
+                for ref in refs[1:]:
+                    total += ref[i].astype(jnp.float32)
+                if put is None:
+                    mine[i] = total.astype(mine.dtype)
+                else:
+                    put(i, total)
+
+            if way == "own":
+                after(h)
+                continue
+            landing, send, recv, who = (
+                (self.from_a, self.a_send, self.a_recv, to_a)
+                if way == "a"
+                else (self.from_b, self.b_send, self.b_recv, to_b)
+            )
+            copy = remote(
+                mine, landing.at[pl.ds(step * self.blocks + h * self.size, self.size)],
+                send.at[step * SPLIT + h], recv.at[step * SPLIT + h], who,
+            )
+            copy.start()
+            self.sent[way, step, h] = copy
+
+    def start(self):
+        for _ in range(AHEAD):
+            self.pair()
+        for j in range(len(self.order)):
+            if self.order[j][1] == 0 and self.order[j][0] != "own":
+                self.chunk(j, lambda: None, None, None)
+
+    def advance(self, work):
+        for j in range(len(self.order) - 1):
+            if self.order[j][1] > 0:
+                self.chunk(j, work, None, None)
+
+    def final(self, store, after=lambda h: None):
+        self.chunk(len(self.order) - 1, lambda: None, store, after)
+
+    def drain(self):
+        for copy in [*self.sent.values(), *self.pairs]:
+            copy.wait_send()
+
+
+class Job:
+    def __init__(self, transposed, plan, blocks, table, running, total, part):
+        self.order, self.keep, self.take, self.last = plan
+        self.blocks, self.table, self.running, self.total, self.part = blocks, table, running, total, part
+        self.contract = ((0,), (0,)) if transposed else ((1,), (0,))
+        self.done = 0
+        self.size = blocks.shape[0] // SLICES
+
+    def slice(self):
+        if self.done == SLICES:
+            return
+        start = self.done * self.size
+        self.done += 1
+
+        def step(i, total):
+            term = lax.dot_general(
+                self.blocks[self.order[start + i]], self.table[self.take[start + i]],
+                (self.contract, ((), ())), preferred_element_type=jnp.float32,
+            )
+            total = jnp.where(self.keep[start + i] == 1, total, 0.0) + term
+            self.running[start + i] = total.astype(self.running.dtype)
+            return total
+
+        self.total[...] = lax.fori_loop(0, self.size, step, self.total[...], unroll=min(4, self.size))
+
+    def finish(self):
+        while self.done < SLICES:
+            self.slice()
+
+        def place(p, unused):
+            self.part[p] = self.running[self.last[p]]
+            return unused
+
+        lax.fori_loop(0, self.part.shape[0], place, 0, unroll=2)
+
+
+def fused_kernel(reg, dev, *refs):
+    forward_plan, backward_plan, refs = refs[:4], refs[4:8], refs[8:]
+    (footprints, probe_matrix, image_out, source_out), refs = refs[:4], refs[4:]
+    blocks, probe, image, part, source_part = refs[0], refs[1:3], refs[3:5], refs[5:7], refs[7:9]
+    running, total, blocks_sem, probe_sem, image_sem = refs[9:14]
+    refs = refs[14:]
+    gathers, scatters = [refs[8 * i : 8 * i + 8] for i in range(4)], [refs[32 + 9 * i : 41 + 9 * i] for i in range(4)]
+    idle = lambda: None
+    ring = Ring(reg, dev)
+    cells = blocks.shape[1]
+    own_probe = ring.chunk(False, 0) * (probe_matrix.shape[0] // cells)
+    own_image = ring.chunk(True, 0) * (image[0].shape[0] // (2 * ring.chips))
+    width = probe_matrix.shape[1] // 2
+    loads = []
+    for h in range(2):
+        for b in range(probe_matrix.shape[0] // cells):
+            copy = pltpu.make_async_copy(
+                probe_matrix.at[pl.ds(b * cells, cells), pl.ds(h * width, width)],
+                probe[h].at[own_probe + b], probe_sem.at[h, b],
+            )
+            copy.start()
+            loads.append(copy)
+    load_blocks = pltpu.make_async_copy(footprints, blocks, blocks_sem)
+    load_blocks.start()
+    ring.barrier()
+    for copy in loads:
+        copy.wait()
+    running[running.shape[0] - 1] = jnp.zeros(running.shape[1:], running.dtype)
+    total[...] = jnp.zeros_like(total)
+
+    spread = [HalfGather(ring, False, probe[h], gathers[h]) for h in range(2)]
+    forward = [Job(False, forward_plan, blocks, probe[h], running, total, part[h]) for h in range(2)]
+    gather = [HalfGather(ring, True, image[h], gathers[2 + h]) for h in range(2)]
+    scatter = [HalfScatter(ring, True, part[h], scatters[h]) for h in range(2)]
+    backward = [Job(True, backward_plan, blocks, image[h], running, total, source_part[h]) for h in range(2)]
+    collect = [HalfScatter(ring, False, source_part[h], scatters[2 + h]) for h in range(2)]
+
+    def start_all(phase):
+        for h in range(SPLIT):
+            phase.start(h)
+
+    def keep_image(h):
+        def store(i, value):
+            image[h][own_image + i] = value.astype(image[h].dtype)
+        return store
+
+    def keep_source(h):
+        def store(i, value):
+            source_out[pl.ds(pl.multiple_of(i * cells, cells), cells), h * width : (h + 1) * width] = value
+        return store
+
+    outs = []
+
+    def write_image(h):
+        count = image_out.shape[0] // cells
+        first = lax.axis_index("dev") * count
+        for b in range(count):
+            copy = pltpu.make_async_copy(
+                image[h].at[first + b],
+                image_out.at[pl.ds(b * cells, cells), pl.ds(h * width, width)], image_sem.at[h, b],
+            )
+            copy.start()
+            outs.append(copy)
+
+    start_all(spread[0])
+    spread[0].advance(idle)
+    start_all(spread[1])
+    spread[0].tail()
+    load_blocks.wait()
+    spread[1].advance(forward[0].slice)
+    forward[0].finish()
+    scatter[0].start()
+    spread[1].tail()
+    scatter[0].advance(forward[1].slice)
+    forward[1].finish()
+    scatter[1].start()
+    scatter[0].final(keep_image(0))
+    scatter[1].advance(idle)
+    start_all(gather[0])
+    scatter[1].final(keep_image(1))
+    gather[0].advance(idle)
+    start_all(gather[1])
+    gather[0].tail()
+    write_image(0)
+    gather[1].advance(backward[0].slice)
+    backward[0].finish()
+    collect[0].start()
+    gather[1].tail()
+    write_image(1)
+    collect[0].advance(backward[1].slice)
+    backward[1].finish()
+    collect[1].start()
+    collect[0].final(keep_source(0))
+    collect[1].advance(idle)
+    collect[1].final(keep_source(1))
+    for phase in (*spread, *scatter, *gather, *collect):
+        phase.drain()
+    for copy in outs:
+        copy.wait()
+
+
+def half_scatter_scratch(chips, blocks, cells, width):
+    half = chips // 2
+    dma = pltpu.SemaphoreType.DMA
+    buffer = lambda n: pltpu.VMEM((n * blocks, cells, width), jnp.bfloat16)
+    return [buffer(chips), buffer(half), buffer(max(half - 1, 1)), dma((chips,)), dma((chips,))] + [
+        dma((half * SPLIT,))
+    ] * 4
+
+
+def fused(reg, dev, forward_plan, backward_plan, footprints, probe_matrix, receptors):
+    count, cells, _ = footprints.shape
+    chips, devices = reg // 2 * dev, reg * dev
+    width = probe_matrix.shape[1] // 2
+    own_sources, own_receptors = probe_matrix.shape[0] // cells, receptors // devices
+    sources = own_sources * devices
+    buffer = lambda n: pltpu.VMEM((n, cells, width), jnp.bfloat16)
+    dma = pltpu.SemaphoreType.DMA
+    scratch = (
+        [pltpu.VMEM(footprints.shape, jnp.bfloat16)]
+        + [buffer(sources)] * 2 + [buffer(receptors)] * 4 + [buffer(sources)] * 2
+        + [buffer(count + 1), pltpu.VMEM((cells, width), jnp.float32)]
+        + [dma(()), dma((2, own_sources)), dma((2, own_receptors * reg))]
+        + gather_scratch(chips)[1:] * 4
+        + half_scatter_scratch(chips, own_receptors, cells, width) * 2
+        + half_scatter_scratch(chips, own_sources, cells, width) * 2
+    )
+    return pl.pallas_call(
+        functools.partial(fused_kernel, reg, dev),
+        out_shape=(
+            jax.ShapeDtypeStruct((receptors // dev * cells, 2 * width), jnp.bfloat16),
+            jax.ShapeDtypeStruct(probe_matrix.shape, jnp.float32),
+        ),
+        in_specs=[pl.BlockSpec(memory_space=pltpu.SMEM)] * 8 + [ANY] * 2,
+        out_specs=(ANY, pl.BlockSpec(memory_space=pltpu.VMEM)),
+        scratch_shapes=scratch,
+        compiler_params=remote_params(4),
+    )(*forward_plan, *backward_plan, footprints, probe_matrix)
+
+
+def with_last(plan, positions):
+    order, keep, pos, take = plan
+    hit = pos[None, :] == jnp.arange(positions, dtype=jnp.int32)[:, None]
+    place = jnp.max(jnp.where(hit, jnp.arange(pos.shape[0], dtype=jnp.int32)[None, :], -1), axis=1)
+    return order, keep, take, jnp.where(place < 0, pos.shape[0], place)
+
+
 def look_up(place, index):
     hit = index[:, None] == jnp.arange(place.shape[0], dtype=jnp.int32)[None, :]
     return jnp.sum(jnp.where(hit, place[None, :], 0), axis=1)
@@ -311,6 +642,15 @@
     pos_src = look_up(source_place, block_coords[:, 1])
     forward_plan = sorted_plan(pos_rec, pos_src)
     backward_plan = sorted_plan(pos_src, pos_rec)
+
+    block_bytes = 2 * cells * columns // 2
+    blocks_held = 2 * (3 * receptors + 3 * sources) + 2 * footprints.shape[0]
+    divides = columns % 256 == 0 and footprints.shape[0] % SLICES == 0
+    if blocks_held * block_bytes <= 48 * 2**20 and divides and chips >= 4:
+        return fused(
+            reg, dev, with_last(forward_plan, receptors), with_last(backward_plan, sources),
+            footprints, probe_matrix, receptors,
+        )
 
     probe_rows = probe_matrix.shape[0]
     probe = pl.pallas_call(

time: 184 us -> 164 us (0.89)
  Pallas kernels: 175 us -> 154 us
    pallas_call x5 -> x1, Pallas kernels: 175 us -> 154 us  [fused(): pl.pallas_call(functools.partial(fused_kernel, reg, dev), out_shape=(jax....]
    dynamic_slice x1 -> x0, local copies, waits for them, and re-layouts: 3.1 us -> none  [local(): lax.dynamic_slice_in_dim(image, lax.axis_index('dev') * reg, reg, 0)]
    unnamed x7 -> x4, local copies, waits for them, and re-layouts: 0.8 us -> 3.9 us
where the time goes in v2:
time: 164 us
  Pallas kernels  154 us (94%)
  other arithmetic  4.78 us (3%)
  local copies, waits for them, and re-layouts  4.66 us (3%)
    pallas_call x1, Pallas kernels, fused(): pl.pallas_call(functools.partial(fused_kernel, reg, dev), out_shape=(jax....  154 us
    unnamed x4, local copies, waits for them, and re-layouts  3.9 us

profile of v2, /device:TPU:0, one launch (start us, length us, event | category | flops | bytes accessed | tf_op | source)
XLA Modules:
  0.0 163.7 jit_solution(14438017591568994711)
XLA Ops:
  0.6 0.8 slice_bitcast_fusion.1
  1.4 0.8 select_reduce_fusion.7
  2.2 0.8 select_reduce_fusion.9
  3.0 0.2 convert_reduce_fusion
  3.2 0.2 convert_reduce_fusion.1
  3.3 0.8 select_reduce_fusion
  4.1 0.1 select_reduce_fusion.3
  4.2 0.6 compare_select_fusion.1.refs_3_
  4.8 0.1 select_reduce_fusion.8
  5.0 0.6 compare_select_fusion.refs_7_
  5.6 0.7 compare_convert_fusion
  6.2 153.6 %shard_map.68 = (bf16[4096,256]{1,0:T(8,128)(2,1)}, f32[512,256]{1,0:T(8,128)}) custom-call(s32[128]{0:T(128)} %get-tuple-element.6.refs_0_, s32[128]{0:T(128)} %get-tuple-element.11.refs_1_, s32[128]{0:T(128)} %get-tuple-element.4.refs_2_, s32[128]{0:T(128)} %compare_select_fusion.1.refs_3_, s32[128]{0:T(128)} %get-tuple-element.7.refs_4_, ...), custom_call_target="tpu_custom_call" | custom-call | tf_op jit(solution)/shard_map/pallas_call | solution.py:595
  159.8 0.0 copy-start
  159.8 3.1 %copy.9 = bf16[4096,256]{1,0:T(8,128)(2,1)} copy(bf16[4096,256]{1,0:T(8,128)(2,1)} %get-tuple-element.14) | data formatting | bytes 4194304
  163.0 0.0 copy-done
  163.0 0.8 copy.10
  (2 shorter events, 0.0 us)
Async XLA Ops:
  159.8 3.1 %copy-start = (f32[512,256]{1,0:T(8,128)S(1)}, f32[512,256]{1,0:T(8,128)}, u32[]{:S(2)}) copy-start(f32[512,256]{1,0:T(8,128)} %get-tuple-element.15) | copy-start | bytes 1572868

commit v3 on v2

--- a/solution.py
+++ b/solution.py
@@ -11,6 +11,7 @@
 ANY = pl.BlockSpec(memory_space=pl.ANY)
 VMEM_LIMIT = 60 * 2**20
 SPLIT = 2
+PIECES = 4
 SLICES = 16
 AHEAD = 3
 
@@ -287,7 +288,7 @@
     def __init__(self, ring, by_dev, full, scratch):
         self.ring, self.by_dev, self.full, self.sems = ring, by_dev, full, scratch
         self.blocks = full.shape[0] // (2 * ring.chips)
-        self.size = self.blocks // SPLIT
+        self.size = self.blocks // PIECES
         self.sent = {}
 
     def send(self, way, step, h):
@@ -296,7 +297,7 @@
         first = ring.chunk(self.by_dev, steps) * self.blocks + h * self.size
         piece = self.full.at[pl.ds(first, self.size)]
         i = "abpq".index(way)
-        index = step * SPLIT + h
+        index = step * PIECES + h
         copy = remote(
             piece, piece, self.sems[2 * i].at[index], self.sems[2 * i + 1].at[index],
             ring.partners()[min(i, 2)],
@@ -312,7 +313,7 @@
 
     def step(self, step, work):
         half = self.ring.half
-        for h in range(SPLIT):
+        for h in range(PIECES):
             work()
             self.sent["a", step - 1, h].wait_recv()
             if step < half:
@@ -325,8 +326,8 @@
                     self.send("b", step, h)
                 self.send("q", step, h)
 
-    def advance(self, work):
-        for step in range(1, self.ring.half):
+    def advance(self, work, first=1, end=None):
+        for step in range(first, end or self.ring.half):
             self.step(step, work)
 
     def tail(self):
@@ -347,7 +348,7 @@
         self.pair_send, self.pair_recv, self.a_send, self.a_recv, self.b_send, self.b_recv = scratch[3:]
         self.order = order_of_use(ring.half)
         self.blocks = part.shape[0] // (2 * ring.chips)
-        self.size = self.blocks // SPLIT
+        self.size = self.blocks // PIECES
         self.pairs, self.sent = [], {}
 
     def pair(self):
@@ -371,7 +372,7 @@
         self.pairs[j].wait_recv()
         self.pair()
         to_a, to_b, _ = ring.partners()
-        for h in range(SPLIT):
+        for h in range(PIECES):
             first = ring.chunk(self.by_dev, ring.sign * scatter_steps(half, way, step)) * self.blocks
             mine = self.part.at[pl.ds(first + h * self.size, self.size)]
             refs = [mine, self.theirs.at[pl.ds(j * self.blocks + h * self.size, self.size)]]
@@ -404,7 +405,7 @@
             )
             copy = remote(
                 mine, landing.at[pl.ds(step * self.blocks + h * self.size, self.size)],
-                send.at[step * SPLIT + h], recv.at[step * SPLIT + h], who,
+                send.at[step * PIECES + h], recv.at[step * PIECES + h], who,
             )
             copy.start()
             self.sent[way, step, h] = copy
@@ -416,10 +417,9 @@
             if self.order[j][1] == 0 and self.order[j][0] != "own":
                 self.chunk(j, lambda: None, None, None)
 
-    def advance(self, work):
-        for j in range(len(self.order) - 1):
-            if self.order[j][1] > 0:
-                self.chunk(j, work, None, None)
+    def advance(self, work, first=2, end=None):
+        for j in range(first, end or len(self.order) - 1):
+            self.chunk(j, work, None, None)
 
     def final(self, store, after=lambda h: None):
         self.chunk(len(self.order) - 1, lambda: None, store, after)
@@ -452,7 +452,7 @@
             self.running[start + i] = total.astype(self.running.dtype)
             return total
 
-        self.total[...] = lax.fori_loop(0, self.size, step, self.total[...], unroll=min(4, self.size))
+        self.total[...] = lax.fori_loop(0, self.size, step, self.total[...], unroll=self.size)
 
     def finish(self):
         while self.done < SLICES:
@@ -503,7 +503,7 @@
     collect = [HalfScatter(ring, False, source_part[h], scatters[2 + h]) for h in range(2)]
 
     def start_all(phase):
-        for h in range(SPLIT):
+        for h in range(PIECES):
             phase.start(h)
 
     def keep_image(h):
@@ -529,24 +529,29 @@
             copy.start()
             outs.append(copy)
 
+    last = ring.half - 1
+    late = len(scatter[0].order) - 3
     start_all(spread[0])
-    spread[0].advance(idle)
+    spread[0].advance(idle, 1, last)
     start_all(spread[1])
+    spread[0].advance(idle, last)
     spread[0].tail()
     load_blocks.wait()
     spread[1].advance(forward[0].slice)
     forward[0].finish()
     scatter[0].start()
     spread[1].tail()
-    scatter[0].advance(forward[1].slice)
+    scatter[0].advance(forward[1].slice, 2, late)
     forward[1].finish()
     scatter[1].start()
-    scatter[0].final(keep_image(0))
+    scatter[0].advance(idle, late)
+    scatter[0].final(keep_image(0), gather[0].start)
     scatter[1].advance(idle)
-    start_all(gather[0])
+    gather[0].advance(idle, 1, 2)
     scatter[1].final(keep_image(1))
-    gather[0].advance(idle)
+    gather[0].advance(idle, 2, last)
     start_all(gather[1])
+    gather[0].advance(idle, last)
     gather[0].tail()
     write_image(0)
     gather[1].advance(backward[0].slice)
@@ -554,9 +559,10 @@
     collect[0].start()
     gather[1].tail()
     write_image(1)
-    collect[0].advance(backward[1].slice)
+    collect[0].advance(backward[1].slice, 2, late)
     backward[1].finish()
     collect[1].start()
+    collect[0].advance(idle, late)
     collect[0].final(keep_source(0))
     collect[1].advance(idle)
     collect[1].final(keep_source(1))
@@ -571,7 +577,7 @@
     dma = pltpu.SemaphoreType.DMA
     buffer = lambda n: pltpu.VMEM((n * blocks, cells, width), jnp.bfloat16)
     return [buffer(chips), buffer(half), buffer(max(half - 1, 1)), dma((chips,)), dma((chips,))] + [
-        dma((half * SPLIT,))
+        dma((half * PIECES,))
     ] * 4
 
 
@@ -588,7 +594,7 @@
         + [buffer(sources)] * 2 + [buffer(receptors)] * 4 + [buffer(sources)] * 2
         + [buffer(count + 1), pltpu.VMEM((cells, width), jnp.float32)]
         + [dma(()), dma((2, own_sources)), dma((2, own_receptors * reg))]
-        + gather_scratch(chips)[1:] * 4
+        + [dma(((chips // 2 + 1) * PIECES,))] * 32
         + half_scatter_scratch(chips, own_receptors, cells, width) * 2
         + half_scatter_scratch(chips, own_sources, cells, width) * 2
     )
@@ -645,8 +651,10 @@
 
     block_bytes = 2 * cells * columns // 2
     blocks_held = 2 * (3 * receptors + 3 * sources) + 2 * footprints.shape[0]
-    divides = columns % 256 == 0 and footprints.shape[0] % SLICES == 0
-    if blocks_held * block_bytes <= 48 * 2**20 and divides and chips >= 4:
+    per_device = [receptors // devices, sources // devices]
+    divides = all(n % PIECES == 0 for n in per_device)
+    divides = divides and columns % 256 == 0 and footprints.shape[0] % SLICES == 0
+    if blocks_held * block_bytes <= 48 * 2**20 and divides and chips >= 8:
         return fused(
             reg, dev, with_last(forward_plan, receptors), with_last(backward_plan, sources),
             footprints, probe_matrix, receptors,

time: 164 us -> 165 us (level)
  no operation moved by 1% of the time
where the time goes in v3:
time: 165 us; the launch traced here: 164 us
  Pallas kernels  154 us (93%)
  other arithmetic  4.78 us (3%)
  local copies, waits for them, and re-layouts  4.66 us (3%)
    pallas_call x1, Pallas kernels, fused(): pl.pallas_call(functools.partial(fused_kernel, reg, dev), out_shape=(jax....  154 us
    unnamed x4, local copies, waits for them, and re-layouts  3.9 us

profile of v3, /device:TPU:0, one launch (start us, length us, event | category | flops | bytes accessed | tf_op | source)
XLA Modules:
  0.0 164.4 jit_solution(15148276656703083380)
XLA Ops:
  0.6 0.8 slice_bitcast_fusion.1
  1.4 0.8 select_reduce_fusion.7
  2.2 0.8 select_reduce_fusion.9
  3.0 0.2 convert_reduce_fusion
  3.2 0.2 convert_reduce_fusion.1
  3.3 0.8 select_reduce_fusion
  4.1 0.1 select_reduce_fusion.3
  4.2 0.6 compare_select_fusion.1.refs_3_
  4.8 0.1 select_reduce_fusion.8
  5.0 0.6 compare_select_fusion.refs_7_
  5.6 0.7 compare_convert_fusion
  6.2 154.3 %shard_map.68 = (bf16[4096,256]{1,0:T(8,128)(2,1)}, f32[512,256]{1,0:T(8,128)}) custom-call(s32[128]{0:T(128)} %get-tuple-element.6.refs_0_, s32[128]{0:T(128)} %get-tuple-element.11.refs_1_, s32[128]{0:T(128)} %get-tuple-element.4.refs_2_, s32[128]{0:T(128)} %compare_select_fusion.1.refs_3_, s32[128]{0:T(128)} %get-tuple-element.7.refs_4_, ...), custom_call_target="tpu_custom_call" | custom-call | tf_op jit(solution)/shard_map/pallas_call | solution.py:601
  160.5 0.0 copy-start
  160.5 3.1 %copy.9 = bf16[4096,256]{1,0:T(8,128)(2,1)} copy(bf16[4096,256]{1,0:T(8,128)(2,1)} %get-tuple-element.14) | data formatting | bytes 4194304
  163.6 0.0 copy-done
  163.6 0.8 copy.10
  (2 shorter events, 0.0 us)
Async XLA Ops:
  160.5 3.1 %copy-start = (f32[512,256]{1,0:T(8,128)S(1)}, f32[512,256]{1,0:T(8,128)}, u32[]{:S(2)}) copy-start(f32[512,256]{1,0:T(8,128)} %get-tuple-element.15) | copy-start | bytes 1572868
